TPU v7x, 32 devices: a whole 2x2x4 slice. The times are simulated.
32 devices in a mesh: wide: 8 (over y, x, core), blk: 4 (over z).
Axes of the slice: x: 2, y: 2, z: 4, core: 2. Of those that a mesh axis runs over, the one named last changes fastest.
Arguments:
- tokens: bfloat16 [16384, 8192], P(('wide', 'blk')), may hold values from -6 to 6
- base_key_matrix: bfloat16 [8192, 1024], P('blk'), may hold values from -0.0625 to 0.0625
- adapter_down_weights: bfloat16 [256, 64, 8192], P(('wide', 'blk')), may hold values from -0.0625 to 0.0625
- adapter_up_weights: bfloat16 [256, 64, 1024], P(('wide', 'blk')), may hold values from -0.75 to 0.75
- request_adapter_index: int32 [256], P(('wide', 'blk')), may hold values from 0 to 255, as said below
Outputs:
- keys: bfloat16 [16384, 1024], P(('wide', 'blk'))
Inputs may be any that keep to these rules, and one draw needn't show every extreme that they name: `request_adapter_index`: request r lies on device r // 8 of wide+blk; adapter a lies on device a // 8. Each request's adapter lies on a device with the same blk index as the request. Of one device's requests at most 2 have adapters on any one wide index; for every blk index one wide index holds the adapters of exactly 2 requests of every device with that blk index.
All inputs are finite; a program needn't handle non-finite values.
Results may differ from a plain program's by a relative error of at most 0.005.
Values may be sent and summed in bfloat16 or wider, within the bound.
A program may use at most 192 MiB of HBM per device.

v0:
```python
import jax
import jax.numpy as jnp
from jax import lax
from jax.sharding import PartitionSpec as P

SEQ = 64
CAP = 2


def per_device(
    tokens, base_key_matrix, adapter_down_weights, adapter_up_weights, request_adapter_index
):
    wide_count = lax.axis_size("wide")
    block_count = lax.axis_size("blk")
    resident_count = adapter_down_weights.shape[0]
    req_count = request_adapter_index.shape[0]
    width = tokens.shape[1]
    out_width = base_key_matrix.shape[1]
    slot_count = wide_count * CAP
    base = jnp.dot(
        tokens,
        lax.all_gather(base_key_matrix, "blk", axis=0, tiled=True),
        preferred_element_type=jnp.float32,
    )
    owner_wide = request_adapter_index // (resident_count * block_count)
    local_ids = request_adapter_index % resident_count
    positions = jnp.arange(req_count, dtype=jnp.int32)
    same_owner = owner_wide[:, None] == owner_wide[None, :]
    earlier = positions[None, :] < positions[:, None]
    rank = jnp.sum(jnp.where(same_owner & earlier, 1, 0), axis=1).astype(jnp.int32)
    slot_of_req = owner_wide * CAP + rank
    member = slot_of_req[:, None] == jnp.arange(slot_count, dtype=jnp.int32)[None, :]
    valid = jnp.any(member, axis=0)
    source_req = jnp.sum(jnp.where(member, positions[:, None], 0), axis=0)
    slot_local = jnp.where(valid, jnp.take(local_ids, source_req, axis=0), 0)[:, None]
    requests = tokens.reshape(req_count, SEQ, width)
    outgoing = jnp.take(requests, source_req, axis=0)
    arrived, received_adapter_index = (
        lax.all_to_all(outgoing, "wide", split_axis=0, concat_axis=0, tiled=True),
        lax.all_to_all(slot_local, "wide", split_axis=0, concat_axis=0, tiled=True),
    )
    selected_down_weight = jnp.take(adapter_down_weights, received_adapter_index[:, 0], axis=0)
    selected_up_weight = jnp.take(adapter_up_weights, received_adapter_index[:, 0], axis=0)
    shrink = jnp.einsum(
        "sqd,srd->sqr", arrived, selected_down_weight, preferred_element_type=jnp.float32
    ).astype(jnp.bfloat16)
    expand = jnp.einsum(
        "sqr,srk->sqk", shrink, selected_up_weight, preferred_element_type=jnp.float32
    ).astype(jnp.bfloat16)
    returned = lax.all_to_all(expand, "wide", split_axis=0, concat_axis=0, tiled=True)
    delta = jnp.take(returned, slot_of_req, axis=0)
    keys = (base + delta.reshape(tokens.shape[0], out_width).astype(jnp.float32)).astype(
        jnp.bfloat16
    )
    return keys


def solution(mesh):
    return jax.shard_map(
        per_device,
        mesh=mesh,
        in_specs=(
            P(("wide", "blk"), None),
            P("blk", None),
            P(("wide", "blk"), None, None),
            P(("wide", "blk"), None, None),
            P(("wide", "blk")),
        ),
        out_specs=P(("wide", "blk"), None),
        check_vma=False,
    )
```

profile of v0, /device:TPU:0, one launch (start us, length us, event | category | flops | bytes accessed | tf_op | source)
XLA Modules:
  0.0 320.9 jit_solution(11483564231436792549)
XLA Ops:
  6.5 0.0 copy-start
  6.5 0.0 all-gather.2.cloned.1.call-start
  6.5 0.7 all-gather.2.cloned.1.call-update
  7.3 0.7 and_select_fusion
  7.9 0.2 select_reduce_fusion.1
  8.1 0.1 fusion.16
  8.2 0.1 reduce_or.12
  8.3 0.1 select_reduce_fusion
  8.4 0.1 reduce_sum.24
  8.5 0.7 gather_fusion
  9.1 0.1 gather.20
  9.2 0.6 select_select_fusion
  9.8 5.2 %all-to-all-start.1 = ((s32[8,2,1]{1,2,0:T(1,128)}), s32[8,2,1]{1,2,0:T(1,128)S(1)}, u32[]{:S(2)}, u32[]{:S(2)}) async-start(s32[8,2,1]{1,2,0:T(1,128)} %bitcast.3), calls=%async_computation.1 | async-start | bytes 8192 | tf_op jit(solution)/shard_map/all_to_all | solution.py:40
  15.0 12.3 %gather_fusion.3 = bf16[16,64,8192]{2,1,0:T(8,128)(2,1)} fusion(bf16[8,64,8192]{2,1,0:T(8,128)(2,1)} %bitcast.15, s32[1024]{0:T(1024)S(1)} %pad_clamp_fusion.4), kind=kCustom, calls=%fused_computation.clone | custom fusion | bytes 33554496 | tf_op jit(solution)/shard_map/jit(_take)/gather | solution.py:37
  27.4 14.5 %broadcast_select_fusion = bf16[16,64,8192]{2,1,0:T(8,128)(2,1)} fusion(bf16[16,64,8192]{2,1,0:T(8,128)(2,1)} %gather_fusion.3, pred[16]{0:T(512)(128)(4,1)S(1)} %compare_and_fusion.1), kind=kLoop, calls=%fused_computation.8 | loop fusion | flops 8388608 | bytes 33554448 | tf_op jit(solution)/shard_map/jit(_take)/select_n | solution.py:37
  41.9 0.0 all-to-all-done.1
  41.9 5.8 %all-to-all-start = ((bf16[16,64,8192]{2,1,0:T(8,128)(2,1)}), bf16[16,64,8192]{2,1,0:T(8,128)(2,1)}, u32[]{:S(2)}, u32[]{:S(2)}) async-start(bf16[16,64,8192]{2,1,0:T(8,128)(2,1)} %broadcast_select_fusion), calls=%async_computation | async-start | bytes 33554432 | tf_op jit(solution)/shard_map/all_to_all | solution.py:39
  47.6 0.1 all_to_all.14
  47.7 0.5 broadcast.225
  48.2 0.7 reduce.5
  48.9 0.1 squeeze.4
  49.0 0.0 copy-done
  49.0 0.7 gather_fusion.1
  49.7 10.4 %gather_fusion.4 = bf16[16,64,8192]{2,1,0:T(8,128)(2,1)} fusion(bf16[8,64,8192]{2,1,0:T(8,128)(2,1)} %param.9, s32[1024]{0:T(1024)S(1)} %pad_clamp_fusion.2), kind=kCustom, calls=%fused_computation.1.clone | custom fusion | bytes 33554496 | tf_op jit(solution)/shard_map/jit(_take)/gather | solution.py:42
  60.1 171.4 %all-to-all-done = bf16[16,64,8192]{2,1,0:T(8,128)(2,1)} async-done(((bf16[16,64,8192]{2,1,0:T(8,128)(2,1)}), bf16[16,64,8192]{2,1,0:T(8,128)(2,1)}, u32[]{:S(2)}, u32[]{:S(2)}) %all-to-all-start) | async-done | bytes 16777248 | tf_op jit(solution)/shard_map/all_to_all | solution.py:39
  231.6 14.6 %fusion.7 = bf16[16,64,1024]{2,1,0:T(8,128)(2,1)} fusion(bf16[16,64,1024]{2,1,0:T(8,128)(2,1)S(1)} %gather_fusion.1, pred[16]{0:T(512)(128)(4,1)S(1)} %compare_and_fusion, bf16[16,64,8192]{2,1,0:T(8,128)(2,1)} %all-to-all-done, bf16[16,64,8192]{2,1,0:T(8,128)(2,1)} %gather_fusion.4), kind=kOutput, calls=%fused_computation.14 | convolution fusion | flops 1218510848 | bytes 37748752 | tf_op jit(solution)/shard_map/sqr,srk->sqk/dot_general | solution.py:47
  246.2 3.6 %all-to-all-start.2 = ((bf16[16,64,1024]{2,1,0:T(8,128)(2,1)}), bf16[16,64,1024]{2,1,0:T(8,128)(2,1)S(1)}, u32[]{:S(2)}, u32[]{:S(2)}) async-start(bf16[16,64,1024]{2,1,0:T(8,128)(2,1)} %fusion.7), calls=%async_computation.2 | async-start | bytes 4194304 | tf_op jit(solution)/shard_map/all_to_all | solution.py:50
  249.8 0.1 broadcast_in_dim.69
  249.8 0.1 broadcast_in_dim.70
  249.9 26.4 %all-to-all-done.2 = bf16[16,64,1024]{2,1,0:T(8,128)(2,1)S(1)} async-done(((bf16[16,64,1024]{2,1,0:T(8,128)(2,1)}), bf16[16,64,1024]{2,1,0:T(8,128)(2,1)S(1)}, u32[]{:S(2)}, u32[]{:S(2)}) %all-to-all-start.2) | async-done | bytes 2097184 | tf_op jit(solution)/shard_map/all_to_all | solution.py:50
  276.3 1.6 gather_fusion.2
  277.9 1.4 bitcast_select_fusion
  279.3 19.1 %all-gather.2.cloned.1.call-done = bf16[8192,1024]{1,0:T(8,128)(2,1)} async-done(((bf16[2048,1024]{1,0:T(8,128)(2,1)}), bf16[8192,1024]{1,0:T(8,128)(2,1)}) %all-gather.2.cloned.1.call-update) | async-done | bytes 16777232 | tf_op jit(solution)/shard_map/all_gather | solution.py:22
  298.4 15.6 %add_convert_fusion = bf16[512,1024]{1,0:T(8,128)(2,1)} fusion(bf16[512,1024]{1,0:T(8,128)(2,1)S(1)} %bitcast_select_fusion, bf16[512,8192]{1,0:T(8,128)(2,1)} %param.7, bf16[8192,1024]{1,0:T(8,128)(2,1)} %all-gather.2.cloned.1.call-done), kind=kOutput, calls=%fused_computation.10 | convolution fusion | flops 8591507456 | bytes 27262976 | tf_op jit(solution)/shard_map/dot_general | solution.py:20
  (13 shorter events, 0.1 us)
Async XLA Ops:
  6.5 42.4 %copy-start = (bf16[8,64,1024]{2,1,0:T(8,128)(2,1)S(1)}, bf16[8,64,1024]{2,1,0:T(8,128)(2,1)}, u32[]{:S(2)}) copy-start(bf16[8,64,1024]{2,1,0:T(8,128)(2,1)} %param.10) | copy-start | bytes 3145732
  6.5 291.9 %all-gather.2.cloned.1.call-start = ((), (), s32[]{:S(2)}) async-start(), calls=%async_computation.3 | async-start | bytes 20971520 | tf_op jit(solution)/shard_map/all_gather | solution.py:22
  9.8 32.0 %all-to-all-start.1 = ((s32[8,2,1]{1,2,0:T(1,128)}), s32[8,2,1]{1,2,0:T(1,128)S(1)}, u32[]{:S(2)}, u32[]{:S(2)}) async-start(s32[8,2,1]{1,2,0:T(1,128)} %bitcast.3), calls=%async_computation.1 | async-start | bytes 8192 | tf_op jit(solution)/shard_map/all_to_all | solution.py:40
  41.9 189.7 %all-to-all-start = ((bf16[16,64,8192]{2,1,0:T(8,128)(2,1)}), bf16[16,64,8192]{2,1,0:T(8,128)(2,1)}, u32[]{:S(2)}, u32[]{:S(2)}) async-start(bf16[16,64,8192]{2,1,0:T(8,128)(2,1)} %broadcast_select_fusion), calls=%async_computation | async-start | bytes 33554432 | tf_op jit(solution)/shard_map/all_to_all | solution.py:39
  246.2 30.2 %all-to-all-start.2 = ((bf16[16,64,1024]{2,1,0:T(8,128)(2,1)}), bf16[16,64,1024]{2,1,0:T(8,128)(2,1)S(1)}, u32[]{:S(2)}, u32[]{:S(2)}) async-start(bf16[16,64,1024]{2,1,0:T(8,128)(2,1)} %fusion.7), calls=%async_computation.2 | async-start | bytes 4194304 | tf_op jit(solution)/shard_map/all_to_all | solution.py:50
Sparse Core Ops, SparseCore 0:
  8.9 289.4 all-gather.1
where the time goes:
time: 321 us
  waiting for transfers between devices  218 us (68%)
  matrix products  30.2 us (9%)
  local copies, waits for them, and re-layouts  26.8 us (8%)
  other arithmetic  18.2 us (6%)
  starting transfers between devices  14.5 us (5%)
  between operations  13.5 us (4%)
    all_to_all x1, waiting for transfers between devices, per_device(): lax.all_to_all(outgoing, 'wide', split_axis=0, concat_axis=0, tiled=True)  171 us
    all_to_all x1, waiting for transfers between devices, per_device(): lax.all_to_all(expand, 'wide', split_axis=0, concat_axis=0, tiled=True)  26.4 us
    all_gather x1, waiting for transfers between devices, per_device(): lax.all_gather(base_key_matrix, 'blk', axis=0, tiled=True)  19.1 us
    dot_general x1, matrix products, per_device(): jnp.dot(tokens, lax.all_gather(base_key_matrix, 'blk', axis=0, tiled=True...  15.6 us
    dot_general x1, matrix products, per_device(): jnp.einsum('sqr,srk->sqk', shrink, selected_up_weight, preferred_element_...  14.6 us
    select_n x2, other arithmetic, per_device(): outgoing = jnp.take(requests, source_req, axis=0)  14.5 us
    gather x1, local copies, waits for them, and re-layouts, per_device(): outgoing = jnp.take(requests, source_req, axis=0)  12.3 us
    gather x1, local copies, waits for them, and re-layouts, per_device(): jnp.take(adapter_down_weights, received_adapter_index[:, 0], axis=0)  10.4 us
  transfers between devices with their start and end apart: 4, of which 3 were waited for; matrix products, arithmetic and copies ran while one was open for 19% of the time, Pallas kernels for 0%

commit v1 on v0

--- a/solution.py
+++ b/solution.py
@@ -5,6 +5,27 @@
 
 SEQ = 64
 CAP = 2
+
+
+def ring_gather(x, axis, dim):
+    size, here, width = (lax.axis_size(axis), lax.axis_index(axis), x.shape[dim])
+    ahead = [(i, (i + 1) % size) for i in range(size)]
+    left = [(i, (i - 1) % size) for i in range(size)]
+    whole = jnp.zeros((*x.shape[:dim], size * width, *x.shape[dim + 1 :]), x.dtype)
+    whole = lax.dynamic_update_slice_in_dim(whole, x, here * width, axis=dim)
+    from_left = from_right = x
+    middle = size // 2
+    for step in range(1, middle + 1):
+        from_left = lax.ppermute(from_left, axis, ahead)
+        whole = lax.dynamic_update_slice_in_dim(
+            whole, from_left, (here - step) % size * width, axis=dim
+        )
+        if step < size - middle:
+            from_right = lax.ppermute(from_right, axis, left)
+            whole = lax.dynamic_update_slice_in_dim(
+                whole, from_right, (here + step) % size * width, axis=dim
+            )
+    return whole
 
 
 def per_device(
@@ -18,9 +39,7 @@
     out_width = base_key_matrix.shape[1]
     slot_count = wide_count * CAP
     base = jnp.dot(
-        tokens,
-        lax.all_gather(base_key_matrix, "blk", axis=0, tiled=True),
-        preferred_element_type=jnp.float32,
+        tokens, ring_gather(base_key_matrix, "blk", 0), preferred_element_type=jnp.float32
     )
     owner_wide = request_adapter_index // (resident_count * block_count)
     local_ids = request_adapter_index % resident_count

time: 321 us -> 341 us (1.062)
  local copies, waits for them, and re-layouts: 26.8 us -> 48.5 us
  between operations: 13.5 us -> 0.17 us
  waiting for transfers between devices: 218 us -> 228 us
  starting transfers between devices: 14.5 us -> 18.6 us
    ppermute x0 -> x3, waiting for transfers between devices: none -> 145 us  [the longest x2 145 us: ring_gather(): from_left = lax.ppermute(from_left, axis, ahead)]
    all_to_all x1, waiting for transfers between devices: 171 us -> 77.9 us  [per_device(): lax.all_to_all(outgoing, 'wide', split_axis=0, concat_axis=0, tiled=True)]
    all_to_all x1, waiting for transfers between devices: 26.4 us -> 0.01 us  [per_device(): lax.all_to_all(expand, 'wide', split_axis=0, concat_axis=0, tiled=True)]
    all_gather x1 -> x0, waiting for transfers between devices: 19.1 us -> none  [per_device(): lax.all_gather(base_key_matrix, 'blk', axis=0, tiled=True)]
    dynamic_update_slice x0 -> x4, local copies, waits for them, and re-layouts: none -> 16.1 us  [the longest x2 9.14 us: ring_gather(): lax.dynamic_update_slice_in_dim(whole, from_left, (here - step) % size *...]
    broadcast_in_dim x0 -> x1, local copies, waits for them, and re-layouts: none -> 6.63 us  [ring_gather(): jnp.zeros((*x.shape[:dim], size * width, *x.shape[dim + 1:]), x.dtype)]
    all_to_all x1, waiting for transfers between devices: 0.01 us -> 4.58 us  [per_device(): lax.all_to_all(slot_local, 'wide', split_axis=0, concat_axis=0, tiled=True)]
    ppermute x0 -> x3, starting transfers between devices: none -> 3.88 us  [the longest x1 2.25 us: ring_gather(): from_right = lax.ppermute(from_right, axis, left)]
  transfers between devices with their start and end apart: 4 -> 6, of which waited for: 3 -> 4; matrix products, arithmetic and copies ran while one was open for 19% -> 14% of each run, Pallas kernels for 0% -> 0%
where the time goes in v1:
time: 341 us
  waiting for transfers between devices  228 us (67%)
  local copies, waits for them, and re-layouts  48.5 us (14%)
  matrix products  29.6 us (9%)
  starting transfers between devices  18.6 us (5%)
  other arithmetic  16.6 us (5%)
    ppermute x2, waiting for transfers between devices, ring_gather(): from_left = lax.ppermute(from_left, axis, ahead)  145 us
    all_to_all x1, waiting for transfers between devices, per_device(): lax.all_to_all(outgoing, 'wide', split_axis=0, concat_axis=0, tiled=True)  77.9 us
    dot_general x1, matrix products, per_device(): jnp.dot(tokens, ring_gather(base_key_matrix, 'blk', 0), preferred_element...  15 us
    dot_general x1, matrix products, per_device(): jnp.einsum('sqr,srk->sqk', shrink, selected_up_weight, preferred_element_...  14.6 us
    select_n x1, other arithmetic, per_device(): outgoing = jnp.take(requests, source_req, axis=0)  14.1 us
    gather x1, local copies, waits for them, and re-layouts, per_device(): outgoing = jnp.take(requests, source_req, axis=0)  10.4 us
    gather x1, local copies, waits for them, and re-layouts, per_device(): jnp.take(adapter_down_weights, received_adapter_index[:, 0], axis=0)  10.4 us
    dynamic_update_slice x2, local copies, waits for them, and re-layouts, ring_gather(): lax.dynamic_update_slice_in_dim(whole, from_left, (here - step) % size *...  9.14 us
  transfers between devices with their start and end apart: 6, of which 4 were waited for; matrix products, arithmetic and copies ran while one was open for 14% of the time, Pallas kernels for 0%

profile of v1, /device:TPU:0, one launch (start us, length us, event | category | flops | bytes accessed | tf_op | source)
XLA Modules:
  0.0 340.9 jit_solution(1150056410798482083)
XLA Ops:
  0.0 0.0 copy-start
  0.0 0.8 and_select_fusion
  0.8 0.2 select_reduce_fusion.1
  1.0 0.1 select_reduce_fusion
  1.0 0.1 fusion.17
  1.1 0.1 reduce_sum.24
  1.2 0.1 reduce_or.12
  1.3 0.7 gather_fusion
  2.0 0.1 gather.20
  2.0 0.6 select_select_fusion
  2.7 5.2 %all-to-all-start.1 = ((s32[8,2,1]{1,2,0:T(1,128)}), s32[8,2,1]{1,2,0:T(1,128)S(1)}, u32[]{:S(2)}, u32[]{:S(2)}) async-start(s32[8,2,1]{1,2,0:T(1,128)} %bitcast.4), calls=%async_computation.1 | async-start | bytes 8192 | tf_op jit(solution)/shard_map/all_to_all | solution.py:59
  7.8 4.6 %all-to-all-done.1 = s32[8,2,1]{1,2,0:T(1,128)S(1)} async-done(((s32[8,2,1]{1,2,0:T(1,128)}), s32[8,2,1]{1,2,0:T(1,128)S(1)}, u32[]{:S(2)}, u32[]{:S(2)}) %all-to-all-start.1) | async-done | bytes 96 | tf_op jit(solution)/shard_map/all_to_all | solution.py:59
  12.4 0.5 broadcast.228
  12.9 0.7 reduce.5
  13.6 0.1 squeeze.4
  13.7 10.4 %gather_fusion.3 = bf16[16,64,8192]{2,1,0:T(8,128)(2,1)} fusion(bf16[8,64,8192]{2,1,0:T(8,128)(2,1)} %bitcast.18, s32[1024]{0:T(1024)S(1)} %pad_clamp_fusion.4), kind=kCustom, calls=%fused_computation.clone | custom fusion | bytes 33554496 | tf_op jit(solution)/shard_map/jit(_take)/gather | solution.py:56
  24.1 14.1 %broadcast_select_fusion = bf16[16,64,8192]{2,1,0:T(8,128)(2,1)} fusion(bf16[16,64,8192]{2,1,0:T(8,128)(2,1)} %gather_fusion.3, pred[16]{0:T(512)(128)(4,1)S(1)} %compare_and_fusion.1), kind=kLoop, calls=%fused_computation.8 | loop fusion | flops 8388608 | bytes 33554448 | tf_op jit(solution)/shard_map/jit(_take)/select_n | solution.py:56
  38.3 5.7 %all-to-all-start = ((bf16[16,64,8192]{2,1,0:T(8,128)(2,1)}), bf16[16,64,8192]{2,1,0:T(8,128)(2,1)}, u32[]{:S(2)}, u32[]{:S(2)}) async-start(bf16[16,64,8192]{2,1,0:T(8,128)(2,1)} %broadcast_select_fusion), calls=%async_computation | async-start | bytes 33554432 | tf_op jit(solution)/shard_map/all_to_all | solution.py:58
  44.0 1.6 collective-permute-start
  45.6 2.2 collective-permute-start.1
  47.9 0.1 all_to_all.14
  48.0 0.0 copy-done
  48.0 0.7 gather_fusion.1
  48.7 90.9 %collective-permute-done = bf16[2048,1024]{1,0:T(8,128)(2,1)} collective-permute-done((bf16[2048,1024]{1,0:T(8,128)(2,1)}, bf16[2048,1024]{1,0:T(8,128)(2,1)}, u32[]{:S(2)}, u32[]{:S(2)}) %collective-permute-start) | collective-permute-done | bytes 4194336 | tf_op jit(solution)/shard_map/ppermute | solution.py:19
  139.6 0.0 collective-permute-start.2
  139.6 10.4 %gather_fusion.4 = bf16[16,64,8192]{2,1,0:T(8,128)(2,1)} fusion(bf16[8,64,8192]{2,1,0:T(8,128)(2,1)} %param.9, s32[1024]{0:T(1024)S(1)} %pad_clamp_fusion.2), kind=kCustom, calls=%fused_computation.1.clone | custom fusion | bytes 33554496 | tf_op jit(solution)/shard_map/jit(_take)/gather | solution.py:61
  150.0 77.9 %all-to-all-done = bf16[16,64,8192]{2,1,0:T(8,128)(2,1)} async-done(((bf16[16,64,8192]{2,1,0:T(8,128)(2,1)}), bf16[16,64,8192]{2,1,0:T(8,128)(2,1)}, u32[]{:S(2)}, u32[]{:S(2)}) %all-to-all-start) | async-done | bytes 16777248 | tf_op jit(solution)/shard_map/all_to_all | solution.py:58
  228.0 14.6 %fusion.8 = bf16[16,64,1024]{2,1,0:T(8,128)(2,1)} fusion(bf16[16,64,1024]{2,1,0:T(8,128)(2,1)S(1)} %gather_fusion.1, pred[16]{0:T(512)(128)(4,1)S(1)} %compare_and_fusion, bf16[16,64,8192]{2,1,0:T(8,128)(2,1)} %all-to-all-done, bf16[16,64,8192]{2,1,0:T(8,128)(2,1)} %gather_fusion.4), kind=kOutput, calls=%fused_computation.15 | convolution fusion | flops 1218510848 | bytes 37748752 | tf_op jit(solution)/shard_map/sqr,srk->sqk/dot_general | solution.py:66
  242.6 3.8 %all-to-all-start.2 = ((bf16[16,64,1024]{2,1,0:T(8,128)(2,1)}), bf16[16,64,1024]{2,1,0:T(8,128)(2,1)S(1)}, u32[]{:S(2)}, u32[]{:S(2)}) async-start(bf16[16,64,1024]{2,1,0:T(8,128)(2,1)} %fusion.8), calls=%async_computation.2 | async-start | bytes 4194304 | tf_op jit(solution)/shard_map/all_to_all | solution.py:69
  246.4 0.1 broadcast_in_dim.73
  246.5 0.1 broadcast_in_dim.74
  246.6 0.0 copy-start.2
  246.6 6.6 %broadcast_in_dim.70 = bf16[8192,1024]{1,0:T(8,128)(2,1)} broadcast(bf16[]{:T(256)} %constant.100.clone.1), dimensions={} | broadcast | bytes 16777218 | tf_op jit(solution)/shard_map/broadcast_in_dim | solution.py:14
  253.2 0.0 copy-done.2
  253.2 2.4 constant_dynamic-update-slice_fusion.3
  255.6 4.6 %constant_dynamic-update-slice_fusion.2 = bf16[8192,1024]{1,0:T(8,128)(2,1)} fusion(bf16[8192,1024]{1,0:T(8,128)(2,1)} %constant_dynamic-update-slice_fusion.3, bf16[2048,1024]{1,0:T(8,128)(2,1)} %collective-permute-done, s32[]{:T(128)S(6)} %select_n.130), kind=kLoop, calls=%fused_computation.43 | loop fusion | bytes 8388612 | tf_op jit(solution)/shard_map/dynamic_update_slice | solution.py:20
  260.2 0.0 collective-permute-done.1
  260.2 4.6 %constant_dynamic-update-slice_fusion.1 = bf16[8192,1024]{1,0:T(8,128)(2,1)} fusion(bf16[8192,1024]{1,0:T(8,128)(2,1)} %constant_dynamic-update-slice_fusion.2, bf16[2048,1024]{1,0:T(8,128)(2,1)} %collective-permute-done.1, s32[]{:T(128)S(6)} %select_n.132), kind=kLoop, calls=%fused_computation.42 | loop fusion | bytes 8388612 | tf_op jit(solution)/shard_map/dynamic_update_slice | solution.py:25
  264.8 54.1 %collective-permute-done.2 = bf16[2048,1024]{1,0:T(8,128)(2,1)} collective-permute-done((bf16[2048,1024]{1,0:T(8,128)(2,1)}, bf16[2048,1024]{1,0:T(8,128)(2,1)}, u32[]{:S(2)}, u32[]{:S(2)}) %collective-permute-start.2) | collective-permute-done | bytes 4194336 | tf_op jit(solution)/shard_map/ppermute | solution.py:19
  318.8 4.6 %constant_dynamic-update-slice_fusion = bf16[8192,1024]{1,0:T(8,128)(2,1)} fusion(bf16[8192,1024]{1,0:T(8,128)(2,1)} %constant_dynamic-update-slice_fusion.1, bf16[2048,1024]{1,0:T(8,128)(2,1)} %collective-permute-done.2, s32[]{:T(128)S(6)} %select_n.134), kind=kLoop, calls=%fused_computation.41 | loop fusion | bytes 8388612 | tf_op jit(solution)/shard_map/dynamic_update_slice | solution.py:20
  323.4 0.0 all-to-all-done.2
  323.4 0.6 gather_fusion.2
  324.0 0.5 copy.14
  324.6 0.0 copy-start.1
  324.6 15.0 %fusion.4 = bf16[512,1024]{0,1:T(8,128)(2,1)S(1)} fusion(bf16[8192,1024]{1,0:T(8,128)(2,1)} %constant_dynamic-update-slice_fusion, bf16[512,8192]{1,0:T(8,128)(2,1)} %param.7, bf16[512,1024]{0,1:T(8,128)(2,1)S(1)} %copy.14, pred[512]{0:T(512)(128)(4,1)S(1)} %broadcast_in_dim.74), kind=kOutput, calls=%fused_computation.11 | convolution fusion | flops 8592031744 | bytes 27263488 | tf_op jit(solution)/shard_map/dot_general | solution.py:41
  339.6 1.3 copy.15
  340.9 0.0 copy-done.1
  (12 shorter events, 0.1 us)
Async XLA Ops:
  0.0 48.0 %copy-start = (bf16[8,64,1024]{2,1,0:T(8,128)(2,1)S(1)}, bf16[8,64,1024]{2,1,0:T(8,128)(2,1)}, u32[]{:S(2)}) copy-start(bf16[8,64,1024]{2,1,0:T(8,128)(2,1)} %param.10) | copy-start | bytes 3145732
  2.7 9.8 %all-to-all-start.1 = ((s32[8,2,1]{1,2,0:T(1,128)}), s32[8,2,1]{1,2,0:T(1,128)S(1)}, u32[]{:S(2)}, u32[]{:S(2)}) async-start(s32[8,2,1]{1,2,0:T(1,128)} %bitcast.4), calls=%async_computation.1 | async-start | bytes 8192 | tf_op jit(solution)/shard_map/all_to_all | solution.py:59
  38.3 189.7 %all-to-all-start = ((bf16[16,64,8192]{2,1,0:T(8,128)(2,1)}), bf16[16,64,8192]{2,1,0:T(8,128)(2,1)}, u32[]{:S(2)}, u32[]{:S(2)}) async-start(bf16[16,64,8192]{2,1,0:T(8,128)(2,1)} %broadcast_select_fusion), calls=%async_computation | async-start | bytes 33554432 | tf_op jit(solution)/shard_map/all_to_all | solution.py:58
  44.0 95.6 %collective-permute-start = (bf16[2048,1024]{1,0:T(8,128)(2,1)}, bf16[2048,1024]{1,0:T(8,128)(2,1)}, u32[]{:S(2)}, u32[]{:S(2)}) collective-permute-start(bf16[2048,1024]{1,0:T(8,128)(2,1)} %param.8), channel_id=1, source_target_pairs={{0,1},{1,2},{2,3},{3,0},{4,5},{5,6},{6,7},{7,4},{8,9},{9,10},{10,1... | collective-permute-start | bytes 12582920 | tf_op jit(solution)/shard_map/ppermute | solution.py:19
  45.6 214.5 %collective-permute-start.1 = (bf16[2048,1024]{1,0:T(8,128)(2,1)}, bf16[2048,1024]{1,0:T(8,128)(2,1)}, u32[]{:S(2)}, u32[]{:S(2)}) collective-permute-start(bf16[2048,1024]{1,0:T(8,128)(2,1)} %param.8), channel_id=1, source_target_pairs={{0,3},{1,0},{2,1},{3,2},{4,7},{5,4},{6,5},{7,6},{8,11},{9,8},{10,9... | collective-permute-start | bytes 12582920 | tf_op jit(solution)/shard_map/ppermute | solution.py:24
  139.6 179.2 %collective-permute-start.2 = (bf16[2048,1024]{1,0:T(8,128)(2,1)}, bf16[2048,1024]{1,0:T(8,128)(2,1)}, u32[]{:S(2)}, u32[]{:S(2)}) collective-permute-start(bf16[2048,1024]{1,0:T(8,128)(2,1)} %collective-permute-done), channel_id=1, source_target_pairs={{0,1},{1,2},{2,3},{3,0},{4,5},{5,6},{6,7},{7,4},{8,9},{9,10},{10,1... | collective-permute-start | bytes 12582920 | tf_op jit(solution)/shard_map/ppermute | solution.py:19
  242.6 80.9 %all-to-all-start.2 = ((bf16[16,64,1024]{2,1,0:T(8,128)(2,1)}), bf16[16,64,1024]{2,1,0:T(8,128)(2,1)S(1)}, u32[]{:S(2)}, u32[]{:S(2)}) async-start(bf16[16,64,1024]{2,1,0:T(8,128)(2,1)} %fusion.8), calls=%async_computation.2 | async-start | bytes 4194304 | tf_op jit(solution)/shard_map/all_to_all | solution.py:69
  246.6 6.6 %copy-start.2 = (bf16[2048,1024]{1,0:T(8,128)(2,1)S(1)}, bf16[2048,1024]{1,0:T(8,128)(2,1)}, u32[]{:S(2)}) copy-start(bf16[2048,1024]{1,0:T(8,128)(2,1)} %param.8) | copy-start | bytes 12582916
  324.6 16.3 %copy-start.1 = (bf16[8,64,1024]{2,1,0:T(8,128)(2,1)S(1)}, bf16[8,64,1024]{2,1,0:T(8,128)(2,1)}, u32[]{:S(2)}) copy-start(bf16[8,64,1024]{2,1,0:T(8,128)(2,1)} %param.10) | copy-start | bytes 3145732
